TPU v7x, 512 devices: a whole 4x8x8 slice. The times are simulated.
512 devices in a mesh: rows: 64 (over z, y), blk: 8 (over x, core).
Axes of the slice: x: 4, y: 8, z: 8, core: 2. Of those that a mesh axis runs over, the one named last changes fastest.
Arguments:
- atom_desc: bfloat16 [1000, 32768], P(None, 'rows'), may hold values from -6 to 6
- sparse_panel: bfloat16 [2048, 1000], P('blk'), may hold values from -0.1875 to 0.1875
- atom_cell: int32 [32768], P('rows'), may hold values from 0 to 31, as said below
- energy_target: bfloat16 [2048], P('rows'), may hold values from -6 to 6
- force_counts: int32 [2048], P('rows'), may hold values from 0 to 1024, as said below
- force_atom: int32 [65536], P('rows'), may hold values from 0 to 511
- force_grad: bfloat16 [1000, 65536], P(None, 'rows'), may hold values from -6 to 6
- force_target: bfloat16 [65536], P('rows'), may hold values from -6 to 6
Outputs:
- gram_matrix: float32 [2048, 2048], P('rows', 'blk')
- right_side: float32 [2048], P('blk')
Inputs may be any that keep to these rules, and one draw needn't show every extreme that they name: `force_counts`: each group's cells together hold at most 1024 force rows; some group holds exactly 1024, all in one of its cells; all groups together hold exactly 512 rows per group on average. `atom_cell`: an index among the cells of the atom's own group. `force_atom`: an index among the atoms of the slot's own group.
All inputs are finite; a program needn't handle non-finite values.
Results may differ from a plain program's by a relative error of at most 0.003.
Values may be sent and summed in bfloat16 or wider, within the bound.
A program may use at most 64 MiB of HBM per device.

v0:
```python
import jax
import jax.numpy as jnp
from jax import lax
from jax.sharding import PartitionSpec as P

CELLS_DEV = 32
FCAP = 1024
FMEAN = 512


def cell_energy(sparse_panel, atom_desc, atom_cell):
    products = jnp.dot(sparse_panel, atom_desc, preferred_element_type=jnp.float32)
    powered = products**4
    member_table = (atom_cell[None, :] == jnp.arange(CELLS_DEV, dtype=jnp.int32)[:, None]).astype(
        jnp.float32
    )
    members = jnp.maximum(jnp.sum(member_table, axis=1), 1.0)
    energy = jnp.dot(powered, member_table.T, precision=lax.Precision.HIGHEST) / members[None, :]
    return (products, energy)


def body(
    atom_desc,
    sparse_panel,
    atom_cell,
    energy_target,
    force_counts,
    force_atom,
    force_grad,
    force_target,
):
    row_devices = lax.axis_size("rows")
    products, energy = cell_energy(sparse_panel, atom_desc, atom_cell)
    live_rows = jnp.sum(force_counts)
    keep_mask = jnp.arange(FCAP, dtype=jnp.int32) < live_rows
    atom_dots = jnp.take(products, force_atom, axis=1)
    grad_dots = jnp.dot(sparse_panel, force_grad, preferred_element_type=jnp.float32)
    forces = jnp.where(keep_mask[None, :], atom_dots**3 * grad_dots, 0.0)
    kernel = jnp.concatenate([energy, forces], axis=1).astype(jnp.bfloat16)
    targets = jnp.concatenate(
        [energy_target, jnp.where(keep_mask, force_target, jnp.zeros_like(force_target))]
    )
    right_part = jnp.dot(kernel, targets, preferred_element_type=jnp.float32)
    right_sum = lax.psum(right_part, "rows")
    rows_all = row_devices * (CELLS_DEV + FMEAN)
    full_kernel = lax.all_gather(kernel, "blk", axis=0, tiled=True)
    owned = lax.psum_scatter(
        lax.dot_general(
            full_kernel, kernel, (((1,), (1,)), ((), ())), preferred_element_type=jnp.float32
        ),
        "rows",
        scatter_dimension=0,
        tiled=True,
    )
    return (owned / rows_all, right_sum / rows_all)


def solution(mesh):
    in_specs = (
        P(None, "rows"),
        P("blk", None),
        P("rows"),
        P("rows"),
        P("rows"),
        P("rows"),
        P(None, "rows"),
        P("rows"),
    )
    out_specs = (P("rows", "blk"), P("blk"))
    return jax.shard_map(body, mesh=mesh, in_specs=in_specs, out_specs=out_specs, check_vma=False)
```

profile of v0, /device:TPU:7, one launch (start us, length us, event | category | flops | bytes accessed | tf_op | source)
XLA Modules:
  0.0 322.0 jit_solution(2896865482038823893)
XLA Ops:
  7.2 0.0 copy-start
  7.2 0.0 all-gather.2.cloned.1.call-start
  7.2 0.8 fusion.6
  8.1 1.3 reduce_sum.19
  9.3 1.3 iota_compare_fusion.2
  10.7 1.8 fusion.7
  12.5 0.2 copy.13
  12.7 4.7 %gather_fusion = f32[1024,256]{1,0:T(8,128)} fusion(f32[256,512]{0,1:T(8,128)S(1)} %copy.13, s32[1024]{0:T(1024)S(1)} %fusion.6), kind=kCustom, calls=%fused_computation | custom fusion | bytes 2101248 | tf_op jit(solution)/shard_map/jit(_take)/gather | solution.py:36
  17.4 2.6 copy.14
  20.0 0.0 copy-done.3
  20.0 0.1 convert_reduce_fusion
  20.2 0.4 fusion.2
  20.6 0.1 copy.15
  20.7 0.0 copy-done
  20.7 0.0 copy-done.2
  20.7 2.0 fusion.1
  22.7 1.1 pad_maximum_fusion
  23.8 0.0 all-gather.2.cloned.1.call-update
  23.8 0.0 reduce-scatter.2.cloned.1.call-start
  23.8 42.9 %all-gather.2.cloned.1.call-done = bf16[2048,1056]{1,0:T(8,128)(2,1)} async-done(((bf16[256,1056]{1,0:T(8,128)(2,1)}), bf16[2048,1056]{1,0:T(8,128)(2,1)}) %all-gather.2.cloned.1.call-update) | async-done | bytes 4325392 | tf_op jit(solution)/shard_map/all_gather | solution.py:46
  66.7 5.4 %fusion.8 = f32[2048,256]{1,0:T(8,128)} fusion(bf16[2048,1056]{1,0:T(8,128)(2,1)} %all-gather.2.cloned.1.call-done, bf16[256,1056]{1,0:T(8,128)(2,1)} %pad_maximum_fusion), kind=kOutput, calls=%fused_computation.23 | convolution fusion | flops 1107296256 | bytes 6963200 | tf_op jit(solution)/shard_map/dot_general | solution.py:48
  72.2 0.0 reduce-scatter.2.cloned.1.call-update
  72.2 0.7 copy-done.4
  72.9 0.6 broadcast_select_fusion
  73.5 0.0 copy-done.5
  73.5 0.1 pad_maximum_fusion.1
  73.6 0.0 copy-done.1
  73.6 0.2 fusion.9
  73.8 116.9 %psum.7 = f32[256]{0:T(256)S(1)} all-reduce(f32[256]{0:T(256)S(1)} %bitcast.11), channel_id=1, replica_groups=mesh['rows'=64,'blk'=8] {'rows'}, use_global_device_ids=true, to_apply=%region_3.4 | all-reduce | flops 256 | bytes 2048 | tf_op jit(solution)/shard_map/psum | solution.py:44
  190.7 0.6 broadcast_multiply_fusion.1
  191.3 122.5 %reduce-scatter.2.cloned.1.call-done = f32[32,256]{1,0:T(8,128)} async-done(((f32[2048,256]{1,0:T(8,128)}), f32[32,256]{1,0:T(8,128)}) %reduce-scatter.2.cloned.1.call-update) | async-done | bytes 32784 | tf_op jit(solution)/shard_map/reduce_scatter | solution.py:47
  313.8 1.4 broadcast_multiply_fusion
  (7 shorter events, 0.0 us)
Async XLA Ops:
  7.2 13.5 %copy-start = (bf16[1000,1024]{1,0:T(8,128)(2,1)S(1)}, bf16[1000,1024]{1,0:T(8,128)(2,1)}, u32[]{:S(2)}) copy-start(bf16[1000,1024]{1,0:T(8,128)(2,1)} %param.14) | copy-start | bytes 6144004
  7.2 59.6 %all-gather.2.cloned.1.call-start = ((), (), s32[]{:S(2)}) async-start(), calls=%async_computation.1 | async-start | bytes 5308416 | tf_op jit(solution)/shard_map/all_gather | solution.py:46
  17.4 2.6 copy-start.3
  17.4 3.3 %copy-start.2 = (bf16[256,1000]{0,1:T(8,128)(2,1)S(1)}, bf16[256,1000]{0,1:T(8,128)(2,1)}, u32[]{:S(2)}) copy-start(bf16[256,1000]{0,1:T(8,128)(2,1)} %param.9) | copy-start | bytes 1536004
  23.8 290.0 %reduce-scatter.2.cloned.1.call-start = ((), (), s32[]{:S(2)}) async-start(), calls=%async_computation.2 | async-start | bytes 2129920 | tf_op jit(solution)/shard_map/reduce_scatter | solution.py:47
  72.2 0.7 copy-start.4
  72.2 1.3 copy-start.5
  72.2 1.4 copy-start.1
Sparse Core Ops, SparseCore 0:
  23.9 42.7 all-gather.1
  72.3 241.3 reduce-scatter.1
where the time goes:
time: 327 us; the launch traced here: 322 us
  waiting for transfers between devices  165 us (50%)
  blocking collectives  117 us (36%)
  between operations  14.1 us (4%)
  matrix products  9.85 us (3%)
  local copies, waits for them, and re-layouts  8.3 us (3%)
  other arithmetic  7.33 us (2%)
    reduce_scatter x1, waiting for transfers between devices, body(): lax.psum_scatter(lax.dot_general(full_kernel, kernel, (((1,), (1,)), ((),...  123 us
    psum x1, blocking collectives, body(): right_sum = lax.psum(right_part, 'rows')  117 us
    all_gather x1, waiting for transfers between devices, body(): full_kernel = lax.all_gather(kernel, 'blk', axis=0, tiled=True)  42.9 us
    gather x2, local copies, waits for them, and re-layouts, body(): atom_dots = jnp.take(products, force_atom, axis=1)  7.3 us
  transfers between devices with their start and end apart: 2, of which 2 were waited for; matrix products, arithmetic and copies ran while one was open for 0% of the time, Pallas kernels for 0%

commit v1 on v0

v1 whole, which is shorter than its diff:
```python
import jax
import jax.numpy as jnp
from jax import lax
from jax.experimental import pallas as pl
from jax.experimental.pallas import tpu as pltpu
from jax.sharding import PartitionSpec as P

MESH = pl.DeviceIdType.MESH
F32, BF16 = jnp.float32, jnp.bfloat16
D, PTS, ATOMS, CELLS, SLOTS = 1000, 256, 512, 32, 1024
COLS = SLOTS + CELLS
ROWS_ALL = 34816.0
NN = (((1,), (0,)), ((), ()))
NT = (((1,), (1,)), ((), ()))


def dot(a, b, dims):
    return lax.dot_general(a, b, dims, preferred_element_type=F32)


def halves(value):
    high = value.astype(BF16)
    return high, (value - high.astype(F32)).astype(BF16)


def kernel(
    desc_hbm, panel_hbm, cell_ref, etarget_ref, counts_ref, fatom_ref, grad_hbm, ftarget_ref,
    gram_ref, right_ref,
    desc, grad, panel_t, panel, hot, member, kern, target, part1, recv1, part2, recv2,
    rpart, rz, rsum, ry,
    load_sem, x_send, x_recv, f_send, f_recv, d_send, d_recv, s1_send, s1_recv, s2_send, s2_recv,
    rz_send, rz_recv, ry_send, ry_recv, token,
):
    r, b = lax.axis_index("rows"), lax.axis_index("blk")
    z, y, x, c = r // 8, r % 8, b // 2, b % 2

    def dev(dz=0, dy=0, dx=0, dc=0):
        return ((z + dz) % 8) * 8 + (y + dy) % 8, ((x + dx) % 4) * 2 + (c + dc) % 2

    def remote(src, dst, send, recv, to):
        return pltpu.make_async_remote_copy(
            src_ref=src, dst_ref=dst, send_sem=send, recv_sem=recv, device_id=to, device_id_type=MESH
        )

    def arrived(ref, sem):
        pltpu.make_async_copy(ref, ref, sem).wait()

    partners = [dev(dc=1), dev(dx=2)]
    partners += [dev(dx=dx, dc=dc) for dx in (1, 3) for dc in (0, 1)]
    partners += [dev(dz=k) for k in range(1, 8)] + [dev(dy=k) for k in range(1, 8)]
    barrier = pltpu.get_barrier_semaphore()
    for partner in partners:
        pl.semaphore_signal(barrier, inc=1, device_id=partner, device_id_type=MESH)
    loads = [
        pltpu.make_async_copy(panel_hbm, panel_t, load_sem.at[0]),
        pltpu.make_async_copy(desc_hbm, desc, load_sem.at[1]),
        pltpu.make_async_copy(grad_hbm, grad, load_sem.at[2]),
    ]
    for load in loads:
        load.start()
    loads[0].wait()
    panel[0] = panel_t[...].T
    pl.semaphore_wait(barrier, len(partners))

    quarter = ((y + 2 * z) % 4) * 64
    sends = []
    for j in (1, 2):
        for h in (0, 1):
            rows = pl.ds(pl.multiple_of(quarter + 32 * h, 32), 32)
            copy = remote(panel.at[0, rows], panel.at[j, rows], x_send.at[j, h], x_recv.at[j, h], dev(dx=-j))
            copy.start()
            sends.append(copy)

    live = jnp.sum(counts_ref[...], axis=1, keepdims=True)
    keep = lax.broadcasted_iota(jnp.int32, (1, SLOTS), 1) < live
    slot_atom = jnp.where(keep, fatom_ref[...], -1)
    atoms = lax.broadcasted_iota(jnp.int32, (ATOMS, SLOTS), 0)
    hot[...] = jnp.where(atoms == slot_atom, 1.0, 0.0).astype(BF16)
    cells = lax.broadcasted_iota(jnp.int32, (CELLS, ATOMS), 0)
    member[...] = jnp.where(cells == cell_ref[...], 1.0, 0.0).astype(BF16)
    masked = jnp.where(keep, ftarget_ref[...].astype(F32), 0.0)
    target[:, :SLOTS] = jnp.broadcast_to(masked, (16, SLOTS)).astype(BF16)
    target[:, SLOTS:] = jnp.broadcast_to(etarget_ref[...].astype(F32), (16, CELLS)).astype(BF16)
    members = dot(jnp.ones((16, ATOMS), BF16), member[...], NT)[0:1]
    members = jnp.maximum(members, 1.0)
    loads[1].wait()
    loads[2].wait()

    def make_rows(j):
        points = panel[j]
        products = dot(points, desc[...], NN)
        high, low = halves(products)
        atom_dots = dot(high, hot[...], NN) + dot(low, hot[...], NN)
        grad_dots = dot(points, grad[...], NN)
        kern[j, c, :, :SLOTS] = (atom_dots * atom_dots * atom_dots * grad_dots).astype(BF16)
        squares = products * products
        high, low = halves(squares * squares)
        energy = dot(high, member[...], NT) + dot(low, member[...], NT)
        kern[j, c, :, SLOTS:] = (energy / members).astype(BF16)
        copy = remote(kern.at[j, c], kern.at[j, c], d_send.at[j], d_recv.at[j], dev(dc=1))
        copy.start()
        sends.append(copy)

    def multiply(j):
        arrived(kern.at[j, 1 - c], d_recv.at[j])
        for a in (0, 1):
            block = dot(kern[j, a], kern[0, c], NT).astype(BF16)
            if j < 2:
                for h in (0, 1):
                    for w in (0, 1):
                        part1[j, 4 * a + 2 * h + w] = block[128 * h : 128 * h + 128, 128 * w : 128 * w + 128]
            else:
                for q in range(8):
                    for w in (0, 1):
                        at = 32 * (2 * a + w)
                        part1[j, q, at : at + 32] = block[32 * q : 32 * q + 32, 128 * w : 128 * w + 128]
        for k in range(1, 8):
            if j < 2:
                to, piece = dev(dz=k), (z + k) % 8
            else:
                to, piece = dev(dy=k), (y + k) % 8
            copy = remote(part1.at[j, piece], recv1.at[j, k - 1], s1_send.at[j, k - 1], s1_recv.at[j], to)
            copy.start()
            sends.append(copy)

    def forward(j):
        for h in (0, 1):
            rows = pl.ds(pl.multiple_of(quarter + 32 * h, 32), 32)
            arrived(panel.at[j, rows], x_recv.at[j, h])
            for n, to in enumerate((dev(dy=1), dev(dy=-1), dev(dz=1 - 2 * h))):
                copy = remote(panel.at[j, rows], panel.at[j, rows], f_send.at[j, h, n], f_recv.at[j], to)
                copy.start()
                sends.append(copy)

    def gathered(j):
        rest = panel.at[j, pl.ds(0, 192)]
        arrived(rest, f_recv.at[j])

    make_rows(0)
    part = dot(target[...], kern[0, c], NT)[0:8]
    rpart[...] = part
    for k in range(1, 8):
        copy = remote(rpart, rz.at[k - 1], rz_send.at[k - 1], rz_recv, dev(dz=k))
        copy.start()
        sends.append(copy)
    multiply(0)
    forward(1)
    forward(2)
    gathered(1)
    make_rows(1)
    multiply(1)

    arrived(rz, rz_recv)
    total = jnp.zeros((8, PTS), F32)
    for s in range(8):
        slot = (z - s + 7) % 8
        value = rz[jnp.minimum(slot, 6)]
        total = total + jnp.where(slot == 7, part, value)
    rsum[...] = total
    for k in range(1, 8):
        copy = remote(rsum, ry.at[k - 1], ry_send.at[k - 1], ry_recv, dev(dy=k))
        copy.start()
        sends.append(copy)

    gathered(2)
    make_rows(2)
    multiply(2)

    arrived(ry, ry_recv)
    final = jnp.zeros((8, PTS), F32)
    for s in range(8):
        slot = (y - s + 7) % 8
        value = ry[jnp.minimum(slot, 6)]
        final = final + jnp.where(slot == 7, total, value)
    right_ref[...] = final[0:1] / ROWS_ALL
    for dc in (0, 1):
        pl.semaphore_signal(token, inc=1, device_id=dev(dx=-1, dc=dc), device_id_type=MESH)
    pl.semaphore_wait(token, 2)

    local = []

    def deliver(n, src, dst, to):
        here = (to[0] == r) & (to[1] == b)
        copy = remote(src, dst, s2_send.at[n], s2_recv, to)

        @pl.when(here)
        def _():
            pltpu.make_async_copy(src, dst, s2_recv).start()

        @pl.when(jnp.logical_not(here))
        def _():
            copy.start()

        local.append((here, copy))

    def first_sum(j, mine):
        arrived(recv1.at[j], s1_recv.at[j])
        acc = part1[j, mine].astype(F32)
        for k in range(7):
            acc = acc + recv1[j, k].astype(F32)
        return acc

    a, h, w = z // 4, (z // 2) % 2, z % 2
    for j in (0, 1):
        acc = first_sum(j, z)
        part2[j] = acc.astype(BF16)
        block = 2 * ((x + j) % 4) + a
        for k in range(4):
            src = part2.at[j, pl.ds(32 * k, 32)]
            deliver(4 * j + k, src, recv2.at[w, y], (block * 8 + 4 * h + k, b))
        if j == 1:
            part2[3] = acc.T.astype(BF16)
            for k in range(4):
                src = part2.at[3, pl.ds(32 * k, 32)]
                copy = remote(src, recv2.at[h, y], s2_send.at[12 + k], s2_recv, (b * 8 + 4 * w + k, block))
                copy.start()
                sends.append(copy)
    part2[2] = first_sum(2, y).astype(BF16)
    for a2 in (0, 1):
        for w2 in (0, 1):
            n = 2 * a2 + w2
            src = part2.at[2, pl.ds(32 * n, 32)]
            deliver(8 + n, src, recv2.at[w2, z], ((2 * ((x + 2) % 4) + a2) * 8 + y, b))

    arrived(recv2, s2_recv)
    for w2 in (0, 1):
        acc = recv2[w2, 0].astype(F32)
        for s in range(1, 8):
            acc = acc + recv2[w2, s].astype(F32)
        gram_ref[:, 128 * w2 : 128 * w2 + 128] = acc / ROWS_ALL

    for copy in sends:
        copy.wait_send()
    for here, copy in local:

        @pl.when(jnp.logical_not(here))
        def _(copy=copy):
            copy.wait_send()


def body(atom_desc, sparse_panel, atom_cell, energy_target, force_counts, force_atom, force_grad, force_target):
    vmem, any_ = pl.BlockSpec(memory_space=pltpu.VMEM), pl.BlockSpec(memory_space=pl.ANY)
    dma, sem = pltpu.VMEM, pltpu.SemaphoreType.DMA
    gram, right = pl.pallas_call(
        kernel,
        out_shape=(jax.ShapeDtypeStruct((32, PTS), F32), jax.ShapeDtypeStruct((1, PTS), F32)),
        in_specs=[any_, any_, vmem, vmem, vmem, vmem, any_, vmem],
        out_specs=(vmem, vmem),
        scratch_shapes=[
            dma((D, ATOMS), BF16),
            dma((D, SLOTS), BF16),
            dma((D, PTS), BF16),
            dma((3, PTS, D), BF16),
            dma((ATOMS, SLOTS), BF16),
            dma((CELLS, ATOMS), BF16),
            dma((3, 2, PTS, COLS), BF16),
            dma((16, COLS), BF16),
            dma((3, 8, 128, 128), BF16),
            dma((3, 7, 128, 128), BF16),
            dma((4, 128, 128), BF16),
            dma((2, 8, 32, 128), BF16),
            dma((8, PTS), F32),
            dma((7, 8, PTS), F32),
            dma((8, PTS), F32),
            dma((7, 8, PTS), F32),
            sem((3,)),
            sem((3, 2)),
            sem((3, 2)),
            sem((3, 2, 3)),
            sem((3,)),
            sem((3,)),
            sem((3,)),
            sem((3, 7)),
            sem((3,)),
            sem((16,)),
            sem,
            sem((7,)),
            sem,
            sem((7,)),
            sem,
            pltpu.SemaphoreType.REGULAR,
        ],
        compiler_params=pltpu.CompilerParams(
            collective_id=0, has_side_effects=True, vmem_limit_bytes=48 * 2**20
        ),
        name="gram",
    )(
        atom_desc,
        sparse_panel.T,
        atom_cell.reshape(1, ATOMS),
        energy_target.reshape(1, CELLS),
        force_counts.reshape(1, CELLS),
        force_atom.reshape(1, SLOTS),
        force_grad,
        force_target.reshape(1, SLOTS),
    )
    return gram, right.reshape(PTS)


def solution(mesh):
    in_specs = (
        P(None, "rows"),
        P("blk", None),
        P("rows"),
        P("rows"),
        P("rows"),
        P("rows"),
        P(None, "rows"),
        P("rows"),
    )
    out_specs = (P("rows", "blk"), P("blk"))
    return jax.shard_map(body, mesh=mesh, in_specs=in_specs, out_specs=out_specs, check_vma=False)
```

time: 327 us -> 62 us (0.19)
  the two profiles are of different devices: /device:TPU:7 before, /device:TPU:11 now
where the time goes in v1:
time: 62 us; the launch traced here: 61.7 us
  Pallas kernels  52.7 us (85%)
  local copies, waits for them, and re-layouts  8.37 us (13%)
  between operations  0.65 us (1%)
    pallas_call x1, Pallas kernels, body(): pl.pallas_call(kernel, out_shape=(jax.ShapeDtypeStruct((32, PTS), F32), j...  52.7 us
    unnamed x16, local copies, waits for them, and re-layouts  7.68 us

profile of v1, /device:TPU:11, one launch (start us, length us, event | category | flops | bytes accessed | tf_op | source)
XLA Modules:
  0.0 61.7 jit_solution(2707752133694244392)
XLA Ops:
  0.6 0.7 %reshape.26.ftarget_ref = bf16[1,1024]{1,0:T(2,128)(2,1)S(1)} reshape(bf16[1024]{0:T(1024)(128)(2,1)} %param.15) | data formatting | bytes 4096 | tf_op jit(solution)/shard_map/reshape | solution.py:295
  1.3 0.0 copy-start
  1.3 1.6 %copy-done = bf16[1000,1024]{1,0:T(8,128)(2,1)S(1)} copy-done((bf16[1000,1024]{1,0:T(8,128)(2,1)S(1)}, bf16[1000,1024]{1,0:T(8,128)(2,1)}, u32[]{:S(2)}) %copy-start) | copy-done | bytes 2048024
  2.9 0.0 copy-start.1
  2.9 1.2 %copy-done.1 = bf16[1000,512]{1,0:T(8,128)(2,1)S(1)} copy-done((bf16[1000,512]{1,0:T(8,128)(2,1)S(1)}, bf16[1000,512]{1,0:T(8,128)(2,1)}, u32[]{:S(2)}) %copy-start.1) | copy-done | bytes 1024024
  4.1 0.0 copy-start.2
  4.1 1.0 %copy-done.2 = bf16[256,1000]{0,1:T(8,128)(2,1)S(1)} copy-done((bf16[256,1000]{0,1:T(8,128)(2,1)S(1)}, bf16[256,1000]{0,1:T(8,128)(2,1)}, u32[]{:S(2)}) %copy-start.2) | copy-done | bytes 512024
  5.1 0.0 copy-start.3
  5.1 0.7 %copy-done.3 = s32[1024]{0:T(1024)S(1)} copy-done((s32[1024]{0:T(1024)S(1)}, s32[1024]{0:T(1024)}, u32[]{:S(2)}) %copy-start.3) | copy-done | bytes 4120
  5.8 0.0 copy-start.4
  5.8 0.7 %copy-done.4 = s32[512]{0:T(512)S(1)} copy-done((s32[512]{0:T(512)S(1)}, s32[512]{0:T(512)}, u32[]{:S(2)}) %copy-start.4) | copy-done | bytes 2072
  6.5 0.0 copy-start.5
  6.5 0.7 %copy-done.5 = bf16[32]{0:T(256)(128)(2,1)S(1)} copy-done((bf16[32]{0:T(256)(128)(2,1)S(1)}, bf16[32]{0:T(256)(128)(2,1)}, u32[]{:S(2)}) %copy-start.5) | copy-done | bytes 88
  7.2 0.0 copy-start.6
  7.2 0.7 %copy-done.6 = s32[32]{0:T(128)S(1)} copy-done((s32[32]{0:T(128)S(1)}, s32[32]{0:T(128)}, u32[]{:S(2)}) %copy-start.6) | copy-done | bytes 152
  7.8 52.7 %gram.1 = (f32[32,256]{1,0:T(8,128)S(1)}, f32[1,256]{1,0:T(1,128)S(1)}) custom-call(bf16[1000,512]{1,0:T(8,128)(2,1)S(1)} %copy-done.1, bf16[1000,256]{1,0:T(8,128)(2,1)S(1)} %bitcast.6, s32[1,512]{1,0:T(1,128)S(1)} %bitcast.8, bf16[1,32]{1,0:T(2,128)(2,1)S(1)} %bitcast.10, s32[1,32]{1,0:T(1,128)S(1)} %bitcast.11, s32[1,1024]{1,0:T(1,128)S(1)} %bitcast.7, ...), custom_call_target="tpu_custom_call" | custom-call | tf_op jit(solution)/shard_map/gram/pallas_call | solution.py:244
  60.5 0.6 %copy.12 = f32[32,256]{1,0:T(8,128)} copy(f32[32,256]{1,0:T(8,128)S(1)} %get-tuple-element.8) | data formatting | bytes 65536
  61.1 0.6 copy.13
Async XLA Ops:
  1.3 1.6 %copy-start = (bf16[1000,1024]{1,0:T(8,128)(2,1)S(1)}, bf16[1000,1024]{1,0:T(8,128)(2,1)}, u32[]{:S(2)}) copy-start(bf16[1000,1024]{1,0:T(8,128)(2,1)} %grad_hbm.1) | copy-start | bytes 6144004
  2.9 1.2 %copy-start.1 = (bf16[1000,512]{1,0:T(8,128)(2,1)S(1)}, bf16[1000,512]{1,0:T(8,128)(2,1)}, u32[]{:S(2)}) copy-start(bf16[1000,512]{1,0:T(8,128)(2,1)} %desc_hbm.1) | copy-start | bytes 3072004
  4.1 1.0 %copy-start.2 = (bf16[256,1000]{0,1:T(8,128)(2,1)S(1)}, bf16[256,1000]{0,1:T(8,128)(2,1)}, u32[]{:S(2)}) copy-start(bf16[256,1000]{0,1:T(8,128)(2,1)} %param.9) | copy-start | bytes 1536004
  5.1 0.7 %copy-start.3 = (s32[1024]{0:T(1024)S(1)}, s32[1024]{0:T(1024)}, u32[]{:S(2)}) copy-start(s32[1024]{0:T(1024)} %param.13) | copy-start | bytes 12292
  5.8 0.7 %copy-start.4 = (s32[512]{0:T(512)S(1)}, s32[512]{0:T(512)}, u32[]{:S(2)}) copy-start(s32[512]{0:T(512)} %param.10) | copy-start | bytes 6148
  6.5 0.7 %copy-start.5 = (bf16[32]{0:T(256)(128)(2,1)S(1)}, bf16[32]{0:T(256)(128)(2,1)}, u32[]{:S(2)}) copy-start(bf16[32]{0:T(256)(128)(2,1)} %param.11) | copy-start | bytes 196
  7.2 0.7 %copy-start.6 = (s32[32]{0:T(128)S(1)}, s32[32]{0:T(128)}, u32[]{:S(2)}) copy-start(s32[32]{0:T(128)} %param.12) | copy-start | bytes 388

commit v2 on v1

v2 whole, which is shorter than its diff:
```python
import jax
import jax.numpy as jnp
from jax import lax
from jax.experimental import pallas as pl
from jax.experimental.pallas import tpu as pltpu
from jax.sharding import PartitionSpec as P

MESH = pl.DeviceIdType.MESH
F32, BF16 = jnp.float32, jnp.bfloat16
D, PTS, ATOMS, CELLS, SLOTS = 1000, 256, 512, 32, 1024
COLS = SLOTS + CELLS
ROWS_ALL = 34816.0
NN = (((1,), (0,)), ((), ()))
NT = (((1,), (1,)), ((), ()))


def dot(a, b, dims):
    return lax.dot_general(a, b, dims, preferred_element_type=F32)


def halves(value):
    high = value.astype(BF16)
    return high, (value - high.astype(F32)).astype(BF16)


def kernel(
    desc_hbm, panel_hbm, cell_hbm, etarget_hbm, counts_hbm, fatom_hbm, grad_hbm, ftarget_hbm,
    gram_ref, right_ref,
    desc, panel_t, cell_ref, etarget_ref, counts_ref, fatom_ref, grad, ftarget_ref,
    panel, hot, member, kern, target, part1, recv1, part2, recv2,
    rpart, rz, rsum, ry,
    load_sem, x_send, x_recv, f_send, f_recv, d_send, d_recv, s1_send, s1_recv, s2_send, s2_recv,
    rz_send, rz_recv, ry_send, ry_recv, token,
):
    r, b = lax.axis_index("rows"), lax.axis_index("blk")
    z, y, x, c = r // 8, r % 8, b // 2, b % 2

    def dev(dz=0, dy=0, dx=0, dc=0):
        return ((z + dz) % 8) * 8 + (y + dy) % 8, ((x + dx) % 4) * 2 + (c + dc) % 2

    def remote(src, dst, send, recv, to):
        return pltpu.make_async_remote_copy(
            src_ref=src, dst_ref=dst, send_sem=send, recv_sem=recv, device_id=to, device_id_type=MESH
        )

    def arrived(ref, sem):
        pltpu.make_async_copy(ref, ref, sem).wait()

    copies = (
        (panel_hbm, panel_t), (desc_hbm, desc), (grad_hbm, grad), (fatom_hbm, fatom_ref), (counts_hbm, counts_ref),
        (cell_hbm, cell_ref), (etarget_hbm, etarget_ref), (ftarget_hbm, ftarget_ref),
    )
    loads = [pltpu.make_async_copy(src, dst, load_sem.at[n]) for n, (src, dst) in enumerate(copies)]
    for load in loads:
        load.start()
    partners = [dev(dc=1), dev(dx=2)]
    partners += [dev(dx=dx, dc=dc) for dx in (1, 3) for dc in (0, 1)]
    partners += [dev(dz=k) for k in range(1, 8)] + [dev(dy=k) for k in range(1, 8)]
    barrier = pltpu.get_barrier_semaphore()
    for partner in partners:
        pl.semaphore_signal(barrier, inc=1, device_id=partner, device_id_type=MESH)
    loads[0].wait()
    points = panel_t[...].T
    panel[0] = points
    for p in range(8):
        for h in (0, 1):
            panel[3, 128 * h + 16 * p : 128 * h + 16 * p + 16] = points[32 * p + 16 * h : 32 * p + 16 * h + 16]

    for load in loads[3:]:
        load.wait()
    live = jnp.sum(counts_ref[...], axis=1, keepdims=True)
    keep = lax.broadcasted_iota(jnp.int32, (1, SLOTS), 1) < live
    slot_atom = jnp.where(keep, fatom_ref[...], -1)
    atoms = lax.broadcasted_iota(jnp.int32, (ATOMS, SLOTS), 0)
    hot[...] = jnp.where(atoms == slot_atom, 1.0, 0.0).astype(BF16)
    cells = lax.broadcasted_iota(jnp.int32, (CELLS, ATOMS), 0)
    member[...] = jnp.where(cells == cell_ref[...], 1.0, 0.0).astype(BF16)
    ftarget = ftarget_ref[...].astype(F32)
    ftarget = jnp.concatenate([ftarget[k : k + 1] for k in range(8)], axis=1)
    target[:, :SLOTS] = jnp.broadcast_to(jnp.where(keep, ftarget, 0.0), (16, SLOTS)).astype(BF16)
    target[:, SLOTS:] = jnp.broadcast_to(etarget_ref[...].astype(F32), (16, CELLS)).astype(BF16)
    members = dot(jnp.ones((16, ATOMS), BF16), member[...], NT)[0:1]
    members = jnp.maximum(members, 1.0)
    for load in loads[1:3]:
        load.wait()

    def make_rows(j, first, count):
        at, own = (0, c) if j == 0 else (1, j - 1)
        rows = slice(first, first + count)
        points = panel[j, rows]
        products = dot(points, desc[...], NN)
        high, low = halves(products)
        atom_dots = dot(high, hot[...], NN) + dot(low, hot[...], NN)
        grad_dots = dot(points, grad[...], NN)
        kern[at, own, rows, :SLOTS] = (atom_dots * atom_dots * atom_dots * grad_dots).astype(BF16)
        squares = products * products
        high, low = halves(squares * squares)
        energy = dot(high, member[...], NT) + dot(low, member[...], NT)
        kern[at, own, rows, SLOTS:] = (energy / members).astype(BF16)

    sends = []

    def send(src, dst, send_sem, recv_sem, to):
        copy = remote(src, dst, send_sem, recv_sem, to)
        copy.start()
        sends.append(copy)

    quarter = ((1 + c) * y + (2 - c) * z) % 4 * 32

    def share(h):
        return pl.ds(pl.multiple_of(128 * h + quarter, 32), 32)

    def fetch(j, h):
        src = panel.at[0 if j == 1 else 3, share(h)]
        send(src, panel.at[j, share(h)], x_send.at[j - 1, h], x_recv.at[j - 1, h], dev(dx=-j))

    def forward(j, h):
        block = panel.at[j, share(h)]
        arrived(block, x_recv.at[j - 1, h])
        side = 1 - 2 * h
        targets = (dev(dy=1 - c, dz=c), dev(dy=c - 1, dz=-c), dev(dy=c * side, dz=(1 - c) * side))
        for n, to in enumerate(targets):
            send(block, block, f_send.at[j - 1, h, n], f_recv.at[j - 1, h], to)

    def gathered(j, h):
        arrived(panel.at[j, pl.ds(128 * h, 96)], f_recv.at[j - 1, h])

    line = (1 - c) * z + c * y
    cross = c * z + (1 - c) * y

    def multiply(j, h):
        rows = kern[0, c, 128 * h : 128 * h + 128] if j == 0 else kern[1, j - 1, 128 * h : 128 * h + 128]
        for a in (0, 1):
            block = dot(rows, kern[0, a], NT).astype(BF16)
            for w in (0, 1):
                part = block[:, 128 * w : 128 * w + 128]
                if j < 2:
                    part1[j, 4 * h + 2 * a + w] = part
                else:
                    at = 64 * h + 16 * (2 * a + w)
                    for p in range(8):
                        part1[j, p, at : at + 16] = part[16 * p : 16 * p + 16]

    def step1(j):
        for k in range(1, 8):
            piece = (line + k) % 8
            to = dev(dz=(1 - c) * k, dy=c * k)
            send(part1.at[j, piece], recv1.at[j, k - 1], s1_send.at[j, k - 1], s1_recv.at[j], to)

    def step1_half(h):
        rows = pl.ds(64 * h, 64)
        for k in range(1, 8):
            src = part1.at[2, (y + k) % 8, rows]
            send(src, recv1.at[2, k - 1, rows], s1_send.at[2 + h, k - 1], s1_recv.at[2 + h], dev(dy=k))

    make_rows(0, 0, 256)
    part = dot(target[...], kern[0, c], NT)[0:8]
    rpart[...] = part
    pl.semaphore_wait(barrier, len(partners))
    fetch(1, 0)
    fetch(1, 1)
    send(kern.at[0, c], kern.at[0, c], d_send, d_recv, dev(dc=1))
    for k in range(1, 8):
        send(rpart, rz.at[k - 1], rz_send.at[k - 1], rz_recv, dev(dz=k))
    arrived(kern.at[0, 1 - c], d_recv)
    fetch(2, 0)
    fetch(2, 1)
    multiply(0, 0)
    multiply(0, 1)
    step1(0)
    forward(1, 0)
    forward(1, 1)
    forward(2, 0)
    gathered(1, 0)
    make_rows(1, 0, 128)
    forward(2, 1)
    gathered(1, 1)
    make_rows(1, 128, 128)
    multiply(1, 0)
    multiply(1, 1)
    step1(1)

    arrived(rz, rz_recv)
    total = jnp.zeros((8, PTS), F32)
    for s in range(8):
        slot = (z - s + 7) % 8
        value = rz[jnp.minimum(slot, 6)]
        total = total + jnp.where(slot == 7, part, value)
    rsum[...] = total
    for k in range(1, 8):
        send(rsum, ry.at[k - 1], ry_send.at[k - 1], ry_recv, dev(dy=k))

    for half in (0, 1):
        gathered(2, half)
        make_rows(2, 128 * half, 128)
        multiply(2, half)
        step1_half(half)

    arrived(ry, ry_recv)
    final = jnp.zeros((8, PTS), F32)
    for s in range(8):
        slot = (y - s + 7) % 8
        value = ry[jnp.minimum(slot, 6)]
        final = final + jnp.where(slot == 7, total, value)
    right_ref[...] = final[0:1] / ROWS_ALL
    for to in (dev(dc=1), dev(dx=-1), dev(dx=-1, dc=1)):
        pl.semaphore_signal(token, inc=1, device_id=to, device_id_type=MESH)
    pl.semaphore_wait(token, 3)

    local = []

    def deliver(n, src, dst, to):
        here = (to[0] == r) & (to[1] == b)
        copy = remote(src, dst, s2_send.at[n], s2_recv, to)

        @pl.when(here)
        def _():
            pltpu.make_async_copy(src, dst, s2_recv).start()

        @pl.when(jnp.logical_not(here))
        def _():
            copy.start()

        local.append((here, copy))

    def first_sum(j, mine, rows, sem):
        arrived(recv1.at[j, :, rows], sem)
        acc = part1[j, mine, rows].astype(F32)
        for k in range(7):
            acc = acc + recv1[j, k, rows].astype(F32)
        return acc

    h, a, w = line // 4, (line // 2) % 2, line % 2
    for j in (0, 1):
        acc = first_sum(j, line, pl.ds(0, 128), s1_recv.at[j])
        part2[j] = acc.astype(BF16)
        block = 2 * ((x + j) % 4) + c
        for k in range(4):
            src = part2.at[j, pl.ds(32 * k, 32)]
            deliver(4 * j + k, src, recv2.at[w, cross], (block * 8 + 4 * h + k, 2 * x + a))
        if j == 1:
            part2[3] = acc.T.astype(BF16)
            for k in range(4):
                src = part2.at[3, pl.ds(32 * k, 32)]
                to = ((2 * x + a) * 8 + 4 * w + k, block)
                send(src, recv2.at[h, cross], s2_send.at[16 + k], s2_recv, to)
    for half in (0, 1):
        rows = pl.ds(64 * half, 64)
        part2[2, rows] = first_sum(2, y, rows, s1_recv.at[2 + half]).astype(BF16)
        for n in range(4):
            src = part2.at[2, pl.ds(64 * half + 16 * n, 16)]
            dst = recv2.at[n % 2, z, pl.ds(16 * half, 16)]
            deliver(8 + 4 * half + n, src, dst, ((2 * ((x + 2) % 4) + c) * 8 + y, 2 * x + n // 2))

    arrived(recv2, s2_recv)
    for w2 in (0, 1):
        acc = recv2[w2, 0].astype(F32)
        for s in range(1, 8):
            acc = acc + recv2[w2, s].astype(F32)
        gram_ref[:, 128 * w2 : 128 * w2 + 128] = acc / ROWS_ALL

    for copy in sends:
        copy.wait_send()
    for here, copy in local:

        @pl.when(jnp.logical_not(here))
        def _(copy=copy):
            copy.wait_send()


def body(atom_desc, sparse_panel, atom_cell, energy_target, force_counts, force_atom, force_grad, force_target):
    vmem, hbm = pl.BlockSpec(memory_space=pltpu.VMEM), pl.BlockSpec(memory_space=pltpu.HBM)
    dma, sem = pltpu.VMEM, pltpu.SemaphoreType.DMA
    operands = (
        atom_desc,
        sparse_panel.T,
        atom_cell.reshape(1, ATOMS),
        energy_target.reshape(1, CELLS),
        force_counts.reshape(1, CELLS),
        force_atom.reshape(1, SLOTS),
        force_grad,
        force_target.reshape(8, 128),
    )
    gram, right = pl.pallas_call(
        kernel,
        out_shape=(jax.ShapeDtypeStruct((32, PTS), F32), jax.ShapeDtypeStruct((1, PTS), F32)),
        in_specs=[hbm] * 8,
        out_specs=(vmem, vmem),
        scratch_shapes=[
            dma((D, ATOMS), BF16),
            dma((D, PTS), BF16),
            dma((1, ATOMS), jnp.int32),
            dma((1, CELLS), BF16),
            dma((1, CELLS), jnp.int32),
            dma((1, SLOTS), jnp.int32),
            dma((D, SLOTS), BF16),
            dma((8, 128), BF16),
            dma((4, PTS, D), BF16),
            dma((ATOMS, SLOTS), BF16),
            dma((CELLS, ATOMS), BF16),
            dma((2, 2, PTS, COLS), BF16),
            dma((16, COLS), BF16),
            dma((3, 8, 128, 128), BF16),
            dma((3, 7, 128, 128), BF16),
            dma((4, 128, 128), BF16),
            dma((2, 8, 32, 128), BF16),
            dma((8, PTS), F32),
            dma((7, 8, PTS), F32),
            dma((8, PTS), F32),
            dma((7, 8, PTS), F32),
            sem((8,)),
            sem((2, 2)),
            sem((2, 2)),
            sem((2, 2, 3)),
            sem((2, 2)),
            sem,
            sem,
            sem((4, 7)),
            sem((4,)),
            sem((20,)),
            sem,
            sem((7,)),
            sem,
            sem((7,)),
            sem,
            pltpu.SemaphoreType.REGULAR,
        ],
        compiler_params=pltpu.CompilerParams(
            collective_id=0, has_side_effects=True, vmem_limit_bytes=24 * 2**20
        ),
        name="gram",
    )(*[pltpu.with_memory_space_constraint(operand, pltpu.HBM) for operand in operands])
    return gram, right.reshape(PTS)


def solution(mesh):
    in_specs = (
        P(None, "rows"),
        P("blk", None),
        P("rows"),
        P("rows"),
        P("rows"),
        P("rows"),
        P(None, "rows"),
        P("rows"),
    )
    out_specs = (P("rows", "blk"), P("blk"))
    return jax.shard_map(body, mesh=mesh, in_specs=in_specs, out_specs=out_specs, check_vma=False)
```

time: 62 us -> 47.9 us (0.77)
  the two profiles are of different devices: /device:TPU:11 before, /device:TPU:57 now
where the time goes in v2:
time: 47.9 us; the launch traced here: 47.8 us
  Pallas kernels  46 us (96%)
  local copies, waits for them, and re-layouts  1.18 us (2%)
  between operations  0.64 us (1%)
    pallas_call x1, Pallas kernels, body(): pl.pallas_call(kernel, out_shape=(jax.ShapeDtypeStruct((32, PTS), F32), j...  46 us
    unnamed x2, local copies, waits for them, and re-layouts  1.18 us

profile of v2, /device:TPU:57, one launch (start us, length us, event | category | flops | bytes accessed | tf_op | source)
XLA Modules:
  0.0 47.8 jit_solution(6040600476071351801)
XLA Ops:
  0.6 46.0 %gram.1 = (f32[32,256]{1,0:T(8,128)S(1)}, f32[1,256]{1,0:T(1,128)S(1)}) custom-call(bf16[1000,512]{1,0:T(8,128)(2,1)} %desc_hbm.1, bf16[1000,256]{1,0:T(8,128)(2,1)} %bitcast.8, s32[1,512]{1,0:T(1,128)} %bitcast.10, bf16[1,32]{1,0:T(2,128)(2,1)} %bitcast.12, s32[1,32]{1,0:T(1,128)} %bitcast.13, s32[1,1024]{1,0:T(1,128)} %bitcast.9, ...), custom_call_target="tpu_custom_call" | custom-call | tf_op jit(solution)/shard_map/gram/pallas_call | solution.py:284
  46.6 0.6 %copy.12 = f32[32,256]{1,0:T(8,128)} copy(f32[32,256]{1,0:T(8,128)S(1)} %get-tuple-element.8) | data formatting | bytes 65536
  47.2 0.6 %copy.13 = f32[256]{0:T(256)} copy(f32[256]{0:T(256)S(1)} %bitcast.7) | data formatting | bytes 2048

commit v3 on v2

--- a/solution.py
+++ b/solution.py
@@ -47,18 +47,18 @@
         pltpu.make_async_copy(ref, ref, sem).wait()
 
     copies = (
-        (panel_hbm, panel_t), (desc_hbm, desc), (grad_hbm, grad), (fatom_hbm, fatom_ref), (counts_hbm, counts_ref),
-        (cell_hbm, cell_ref), (etarget_hbm, etarget_ref), (ftarget_hbm, ftarget_ref),
+        (panel_hbm, panel_t), (fatom_hbm, fatom_ref), (counts_hbm, counts_ref), (cell_hbm, cell_ref),
+        (etarget_hbm, etarget_ref), (ftarget_hbm, ftarget_ref), (desc_hbm, desc), (grad_hbm, grad),
     )
     loads = [pltpu.make_async_copy(src, dst, load_sem.at[n]) for n, (src, dst) in enumerate(copies)]
-    for load in loads:
-        load.start()
-    partners = [dev(dc=1), dev(dx=2)]
-    partners += [dev(dx=dx, dc=dc) for dx in (1, 3) for dc in (0, 1)]
-    partners += [dev(dz=k) for k in range(1, 8)] + [dev(dy=k) for k in range(1, 8)]
+    loads[0].start()
+    around = [dev(dy=1), dev(dy=-1), dev(dz=1), dev(dz=-1)]
+    partners = [dev(dc=1), dev(dx=2)] + [dev(dx=dx, dc=dc) for dx in (1, 3) for dc in (0, 1)] + around
     barrier = pltpu.get_barrier_semaphore()
     for partner in partners:
         pl.semaphore_signal(barrier, inc=1, device_id=partner, device_id_type=MESH)
+    for load in loads[1:]:
+        load.start()
     loads[0].wait()
     points = panel_t[...].T
     panel[0] = points
@@ -66,7 +66,7 @@
         for h in (0, 1):
             panel[3, 128 * h + 16 * p : 128 * h + 16 * p + 16] = points[32 * p + 16 * h : 32 * p + 16 * h + 16]
 
-    for load in loads[3:]:
+    for load in loads[1:6]:
         load.wait()
     live = jnp.sum(counts_ref[...], axis=1, keepdims=True)
     keep = lax.broadcasted_iota(jnp.int32, (1, SLOTS), 1) < live
@@ -81,9 +81,6 @@
     target[:, SLOTS:] = jnp.broadcast_to(etarget_ref[...].astype(F32), (16, CELLS)).astype(BF16)
     members = dot(jnp.ones((16, ATOMS), BF16), member[...], NT)[0:1]
     members = jnp.maximum(members, 1.0)
-    for load in loads[1:3]:
-        load.wait()
-
     def make_rows(j, first, count):
         at, own = (0, c) if j == 0 else (1, j - 1)
         rows = slice(first, first + count)
@@ -98,7 +95,7 @@
         energy = dot(high, member[...], NT) + dot(low, member[...], NT)
         kern[at, own, rows, SLOTS:] = (energy / members).astype(BF16)
 
-    sends = []
+    sends, local = [], []
 
     def send(src, dst, send_sem, recv_sem, to):
         copy = remote(src, dst, send_sem, recv_sem, to)
@@ -126,75 +123,190 @@
         arrived(panel.at[j, pl.ds(128 * h, 96)], f_recv.at[j - 1, h])
 
     line = (1 - c) * z + c * y
-    cross = c * z + (1 - c) * y
-
-    def multiply(j, h):
-        rows = kern[0, c, 128 * h : 128 * h + 128] if j == 0 else kern[1, j - 1, 128 * h : 128 * h + 128]
+
+    far_first = (4, 3, 5, 2, 6, 1, 7)
+
+    def tell(n):
+        for to in around:
+            pl.semaphore_signal(token.at[n], inc=1, device_id=to, device_id_type=MESH)
+
+    def hear(n):
+        pl.semaphore_wait(token.at[n], len(around))
+
+    def multiply_a():
+        blocks = [dot(kern[0, c], kern[0, a], NT).astype(BF16) for a in (0, 1)]
+        for core, pieces in enumerate((((0, 0), (0, 1), (0, 2), (1, 1), (1, 3)), ((0, 2), (0, 3), (0, 1), (1, 3), (1, 0)))):
+
+            @pl.when(c == core)
+            def _(pieces=pieces):
+                for n, (h, w) in enumerate(pieces):
+                    at = 128 * (w % 2)
+                    part1[0, n] = blocks[w // 2][128 * h : 128 * h + 128, at : at + 128]
+
+    def step1_a():
+        for n in range(5):
+            to = n + 3 * c
+            k = (to - z + 8) % 8
+            here = k == 0
+            slot = jnp.where(here, 0, k - 1)
+            copy = remote(part1.at[0, n], recv1.at[0, slot], s1_send.at[0, n], s1_recv.at[0], dev(dz=to - z + 8))
+
+            @pl.when(jnp.logical_not(here))
+            def _(copy=copy):
+                copy.start()
+
+            local.append((here, copy))
+
+    def multiply_b():
+        for a in (0, 1):
+            block = dot(kern[1, 0], kern[0, a], NT).astype(BF16)
+            for h in (0, 1):
+                for w in (0, 1):
+                    part1[1, 4 * w + 2 * h + a] = block[128 * h : 128 * h + 128, 128 * w : 128 * w + 128]
+
+    def multiply_half(h):
+        rows = kern[1, 1, 128 * h : 128 * h + 128]
         for a in (0, 1):
             block = dot(rows, kern[0, a], NT).astype(BF16)
             for w in (0, 1):
-                part = block[:, 128 * w : 128 * w + 128]
-                if j < 2:
-                    part1[j, 4 * h + 2 * a + w] = part
-                else:
-                    at = 64 * h + 16 * (2 * a + w)
-                    for p in range(8):
-                        part1[j, p, at : at + 16] = part[16 * p : 16 * p + 16]
-
-    def step1(j):
-        for k in range(1, 8):
-            piece = (line + k) % 8
+                at = 64 * h + 16 * (2 * a + w)
+                for p in range(8):
+                    part1[2, p, at : at + 16] = block[16 * p : 16 * p + 16, 128 * w : 128 * w + 128]
+
+    def step1_b():
+        for k in far_first:
             to = dev(dz=(1 - c) * k, dy=c * k)
-            send(part1.at[j, piece], recv1.at[j, k - 1], s1_send.at[j, k - 1], s1_recv.at[j], to)
+            send(part1.at[1, (line + k) % 8], recv1.at[1, k - 1], s1_send.at[1, k - 1], s1_recv.at[1], to)
 
     def step1_half(h):
         rows = pl.ds(64 * h, 64)
-        for k in range(1, 8):
+        for k in far_first:
             src = part1.at[2, (y + k) % 8, rows]
             send(src, recv1.at[2, k - 1, rows], s1_send.at[2 + h, k - 1], s1_recv.at[2 + h], dev(dy=k))
 
-    make_rows(0, 0, 256)
-    part = dot(target[...], kern[0, c], NT)[0:8]
-    rpart[...] = part
     pl.semaphore_wait(barrier, len(partners))
     fetch(1, 0)
     fetch(1, 1)
+    tell(0)
+    for load in loads[6:]:
+        load.wait()
+    make_rows(0, 0, 256)
     send(kern.at[0, c], kern.at[0, c], d_send, d_recv, dev(dc=1))
-    for k in range(1, 8):
-        send(rpart, rz.at[k - 1], rz_send.at[k - 1], rz_recv, dev(dz=k))
-    arrived(kern.at[0, 1 - c], d_recv)
+    hear(0)
+    tell(1)
+    part = dot(target[...], kern[0, c], NT)[0:8]
+    rpart[...] = part
+    forward(1, 0)
     fetch(2, 0)
     fetch(2, 1)
-    multiply(0, 0)
-    multiply(0, 1)
-    step1(0)
-    forward(1, 0)
+    hear(1)
+    tell(2)
     forward(1, 1)
+    arrived(kern.at[0, 1 - c], d_recv)
+    multiply_a()
+    hear(2)
+    for k in far_first:
+        send(rpart, rz.at[k - 1], rz_send.at[k - 1], rz_recv, dev(dz=k))
     forward(2, 0)
     gathered(1, 0)
     make_rows(1, 0, 128)
     forward(2, 1)
+    step1_a()
     gathered(1, 1)
     make_rows(1, 128, 128)
-    multiply(1, 0)
-    multiply(1, 1)
-    step1(1)
+    multiply_b()
+    step1_b()
+
+    gathered(2, 0)
+    make_rows(2, 0, 128)
+    multiply_half(0)
+    step1_half(0)
 
     arrived(rz, rz_recv)
+    for to in (dev(dc=1), dev(dx=-1), dev(dx=-1, dc=1)):
+        pl.semaphore_signal(token.at[3], inc=1, device_id=to, device_id_type=MESH)
     total = jnp.zeros((8, PTS), F32)
     for s in range(8):
         slot = (z - s + 7) % 8
         value = rz[jnp.minimum(slot, 6)]
         total = total + jnp.where(slot == 7, part, value)
     rsum[...] = total
-    for k in range(1, 8):
+    for k in far_first:
         send(rsum, ry.at[k - 1], ry_send.at[k - 1], ry_recv, dev(dy=k))
 
+    gathered(2, 1)
+    make_rows(2, 128, 128)
+    multiply_half(1)
+    step1_half(1)
+
+    pl.semaphore_wait(token.at[3], 3)
+
+    def deliver(n, src, dst, to):
+        here = (to[0] == r) & (to[1] == b)
+        copy = remote(src, dst, s2_send.at[n], s2_recv, to)
+
+        @pl.when(here)
+        def _():
+            pltpu.make_async_copy(src, dst, s2_recv).start()
+
+        @pl.when(jnp.logical_not(here))
+        def _():
+            copy.start()
+
+        return here, copy
+
+    def first_sum(j, mine, rows, sem):
+        arrived(recv1.at[j, :, rows], sem)
+        acc = part1[j, mine, rows].astype(F32)
+        for k in range(7):
+            acc = acc + recv1[j, k, rows].astype(F32)
+        return acc
+
+    n = z - 3 * c
+    down = 2 * c + jnp.where(n >= 3, 1, 0)
+    first = jnp.where(n == 3, 1, jnp.where(n == 4, 3, n))
+    second = jnp.where(n == 0, 2, jnp.where(n == 2, 1, jnp.where(n == 4, 0, 3)))
+    across = jnp.where(c == 0, first, second)
+
+    holds = (n >= 0) & (n < 5)
+    targets_a = [((2 * x + down // 2) * 8 + 4 * (down % 2) + k, 2 * x + across // 2) for k in range(4)]
+    targets_t = [((2 * x + across // 2) * 8 + 4 * (across % 2) + k, 2 * x + down // 2) for k in range(4)]
+
+    @pl.when(holds)
+    def _():
+        acc = first_sum(0, n, pl.ds(0, 128), s1_recv.at[0])
+        part2[0] = acc.astype(BF16)
+        for k in range(4):
+            src = part2.at[0, pl.ds(32 * k, 32)]
+            deliver(8 + k, src, recv2.at[across % 2, y], targets_a[k])
+
+        @pl.when(down != across)
+        def _():
+            part2[4] = acc.T.astype(BF16)
+            for k in range(4):
+                src = part2.at[4, pl.ds(32 * k, 32)]
+                deliver(12 + k, src, recv2.at[down % 2, y], targets_t[k])
+
+    w, h, a = line // 4, (line // 2) % 2, line % 2
+    cross, block = z + y - line, 2 * ((x + 1) % 4) + c
+    acc = first_sum(1, line, pl.ds(0, 128), s1_recv.at[1])
+    part2[1] = acc.astype(BF16)
+    part2[3] = acc.T.astype(BF16)
+    for k in range(4):
+        src = part2.at[3, pl.ds(32 * k, 32)]
+        send(src, recv2.at[h, cross], s2_send.at[k], s2_recv, ((2 * x + a) * 8 + 4 * w + k, block))
+    for k in range(4):
+        src = part2.at[1, pl.ds(32 * k, 32)]
+        local.append(deliver(4 + k, src, recv2.at[w, cross], (block * 8 + 4 * h + k, 2 * x + a)))
+
     for half in (0, 1):
-        gathered(2, half)
-        make_rows(2, 128 * half, 128)
-        multiply(2, half)
-        step1_half(half)
+        rows = pl.ds(64 * half, 64)
+        part2[2, rows] = first_sum(2, y, rows, s1_recv.at[2 + half]).astype(BF16)
+        for n in range(4):
+            src = part2.at[2, pl.ds(64 * half + 16 * n, 16)]
+            dst = recv2.at[n % 2, z, pl.ds(16 * half, 16)]
+            to = ((2 * ((x + 2) % 4) + c) * 8 + y, 2 * x + n // 2)
+            local.append(deliver(16 + 4 * half + n, src, dst, to))
 
     arrived(ry, ry_recv)
     final = jnp.zeros((8, PTS), F32)
@@ -203,54 +315,19 @@
         value = ry[jnp.minimum(slot, 6)]
         final = final + jnp.where(slot == 7, total, value)
     right_ref[...] = final[0:1] / ROWS_ALL
-    for to in (dev(dc=1), dev(dx=-1), dev(dx=-1, dc=1)):
-        pl.semaphore_signal(token, inc=1, device_id=to, device_id_type=MESH)
-    pl.semaphore_wait(token, 3)
-
-    local = []
-
-    def deliver(n, src, dst, to):
-        here = (to[0] == r) & (to[1] == b)
-        copy = remote(src, dst, s2_send.at[n], s2_recv, to)
-
-        @pl.when(here)
-        def _():
-            pltpu.make_async_copy(src, dst, s2_recv).start()
+
+    for k in range(4):
+        for n, src, to, active in ((8, 0, targets_a[k], holds), (12, 4, targets_t[k], holds & (down != across))):
+            here = (to[0] == r) & (to[1] == b)
+            copy = remote(part2.at[src, pl.ds(32 * k, 32)], recv2.at[0, 0], s2_send.at[n + k], s2_recv, to)
+            local.append((here | jnp.logical_not(active), copy))
+    for copy in sends:
+        copy.wait_send()
+    for here, copy in local:
 
         @pl.when(jnp.logical_not(here))
-        def _():
-            copy.start()
-
-        local.append((here, copy))
-
-    def first_sum(j, mine, rows, sem):
-        arrived(recv1.at[j, :, rows], sem)
-        acc = part1[j, mine, rows].astype(F32)
-        for k in range(7):
-            acc = acc + recv1[j, k, rows].astype(F32)
-        return acc
-
-    h, a, w = line // 4, (line // 2) % 2, line % 2
-    for j in (0, 1):
-        acc = first_sum(j, line, pl.ds(0, 128), s1_recv.at[j])
-        part2[j] = acc.astype(BF16)
-        block = 2 * ((x + j) % 4) + c
-        for k in range(4):
-            src = part2.at[j, pl.ds(32 * k, 32)]
-            deliver(4 * j + k, src, recv2.at[w, cross], (block * 8 + 4 * h + k, 2 * x + a))
-        if j == 1:
-            part2[3] = acc.T.astype(BF16)
-            for k in range(4):
-                src = part2.at[3, pl.ds(32 * k, 32)]
-                to = ((2 * x + a) * 8 + 4 * w + k, block)
-                send(src, recv2.at[h, cross], s2_send.at[16 + k], s2_recv, to)
-    for half in (0, 1):
-        rows = pl.ds(64 * half, 64)
-        part2[2, rows] = first_sum(2, y, rows, s1_recv.at[2 + half]).astype(BF16)
-        for n in range(4):
-            src = part2.at[2, pl.ds(64 * half + 16 * n, 16)]
-            dst = recv2.at[n % 2, z, pl.ds(16 * half, 16)]
-            deliver(8 + 4 * half + n, src, dst, ((2 * ((x + 2) % 4) + c) * 8 + y, 2 * x + n // 2))
+        def _(copy=copy):
+            copy.wait_send()
 
     arrived(recv2, s2_recv)
     for w2 in (0, 1):
@@ -258,14 +335,6 @@
         for s in range(1, 8):
             acc = acc + recv2[w2, s].astype(F32)
         gram_ref[:, 128 * w2 : 128 * w2 + 128] = acc / ROWS_ALL
-
-    for copy in sends:
-        copy.wait_send()
-    for here, copy in local:
-
-        @pl.when(jnp.logical_not(here))
-        def _(copy=copy):
-            copy.wait_send()
 
 
 def body(atom_desc, sparse_panel, atom_cell, energy_target, force_counts, force_atom, force_grad, force_target):
@@ -302,7 +371,7 @@
             dma((16, COLS), BF16),
             dma((3, 8, 128, 128), BF16),
             dma((3, 7, 128, 128), BF16),
-            dma((4, 128, 128), BF16),
+            dma((5, 128, 128), BF16),
             dma((2, 8, 32, 128), BF16),
             dma((8, PTS), F32),
             dma((7, 8, PTS), F32),
@@ -317,13 +386,13 @@
             sem,
             sem((4, 7)),
             sem((4,)),
-            sem((20,)),
+            sem((24,)),
             sem,
             sem((7,)),
             sem,
             sem((7,)),
             sem,
-            pltpu.SemaphoreType.REGULAR,
+            pltpu.SemaphoreType.REGULAR((4,)),
         ],
         compiler_params=pltpu.CompilerParams(
             collective_id=0, has_side_effects=True, vmem_limit_bytes=24 * 2**20

time: 47.9 us -> 42.9 us (0.90)
  the two profiles are of different devices: /device:TPU:57 before, /device:TPU:7 now
where the time goes in v3:
time: 42.9 us; the launch traced here: 42.2 us
  Pallas kernels  40.4 us (94%)
  local copies, waits for them, and re-layouts  1.18 us (3%)
  between operations  0.64 us (1%)
    pallas_call x1, Pallas kernels, body(): pl.pallas_call(kernel, out_shape=(jax.ShapeDtypeStruct((32, PTS), F32), j...  40.4 us
    unnamed x2, local copies, waits for them, and re-layouts  1.18 us

profile of v3, /device:TPU:7, one launch (start us, length us, event | category | flops | bytes accessed | tf_op | source)
XLA Modules:
  0.0 42.2 jit_solution(12742036626926804958)
XLA Ops:
  0.6 40.4 %gram.1 = (f32[32,256]{1,0:T(8,128)S(1)}, f32[1,256]{1,0:T(1,128)S(1)}) custom-call(bf16[1000,512]{1,0:T(8,128)(2,1)} %desc_hbm.1, bf16[1000,256]{1,0:T(8,128)(2,1)} %bitcast.8, s32[1,512]{1,0:T(1,128)} %bitcast.10, bf16[1,32]{1,0:T(2,128)(2,1)} %bitcast.12, s32[1,32]{1,0:T(1,128)} %bitcast.13, s32[1,1024]{1,0:T(1,128)} %bitcast.9, ...), custom_call_target="tpu_custom_call" | custom-call | tf_op jit(solution)/shard_map/gram/pallas_call | solution.py:353
  41.0 0.6 %copy.12 = f32[32,256]{1,0:T(8,128)} copy(f32[32,256]{1,0:T(8,128)S(1)} %get-tuple-element.8) | data formatting | bytes 65536
  41.6 0.6 %copy.13 = f32[256]{0:T(256)} copy(f32[256]{0:T(256)S(1)} %bitcast.7) | data formatting | bytes 2048

commit v4 on v3

--- a/solution.py
+++ b/solution.py
@@ -95,12 +95,8 @@
         energy = dot(high, member[...], NT) + dot(low, member[...], NT)
         kern[at, own, rows, SLOTS:] = (energy / members).astype(BF16)
 
-    sends, local = [], []
-
     def send(src, dst, send_sem, recv_sem, to):
-        copy = remote(src, dst, send_sem, recv_sem, to)
-        copy.start()
-        sends.append(copy)
+        remote(src, dst, send_sem, recv_sem, to).start()
 
     quarter = ((1 + c) * y + (2 - c) * z) % 4 * 32
 
@@ -109,15 +105,21 @@
 
     def fetch(j, h):
         src = panel.at[0 if j == 1 else 3, share(h)]
-        send(src, panel.at[j, share(h)], x_send.at[j - 1, h], x_recv.at[j - 1, h], dev(dx=-j))
+        send(src, panel.at[j, share(h)], x_send, x_recv.at[j - 1, h], dev(dx=-j))
+
+    def fetch_c(now):
+        @pl.when(now)
+        def _():
+            fetch(2, 0)
+            fetch(2, 1)
 
     def forward(j, h):
         block = panel.at[j, share(h)]
         arrived(block, x_recv.at[j - 1, h])
         side = 1 - 2 * h
         targets = (dev(dy=1 - c, dz=c), dev(dy=c - 1, dz=-c), dev(dy=c * side, dz=(1 - c) * side))
-        for n, to in enumerate(targets):
-            send(block, block, f_send.at[j - 1, h, n], f_recv.at[j - 1, h], to)
+        for to in targets:
+            send(block, block, f_send, f_recv.at[j - 1, h], to)
 
     def gathered(j, h):
         arrived(panel.at[j, pl.ds(128 * h, 96)], f_recv.at[j - 1, h])
@@ -143,19 +145,17 @@
                     at = 128 * (w % 2)
                     part1[0, n] = blocks[w // 2][128 * h : 128 * h + 128, at : at + 128]
 
-    def step1_a():
+    def step1_a(now):
         for n in range(5):
             to = n + 3 * c
             k = (to - z + 8) % 8
             here = k == 0
             slot = jnp.where(here, 0, k - 1)
-            copy = remote(part1.at[0, n], recv1.at[0, slot], s1_send.at[0, n], s1_recv.at[0], dev(dz=to - z + 8))
-
-            @pl.when(jnp.logical_not(here))
+            copy = remote(part1.at[0, n], recv1.at[0, slot], s1_send.at[0], s1_recv.at[0], dev(dz=to - z + 8))
+
+            @pl.when(jnp.logical_not(here) & now)
             def _(copy=copy):
                 copy.start()
-
-            local.append((here, copy))
 
     def multiply_b():
         for a in (0, 1):
@@ -173,16 +173,18 @@
                 for p in range(8):
                     part1[2, p, at : at + 16] = block[16 * p : 16 * p + 16, 128 * w : 128 * w + 128]
 
-    def step1_b():
-        for k in far_first:
-            to = dev(dz=(1 - c) * k, dy=c * k)
-            send(part1.at[1, (line + k) % 8], recv1.at[1, k - 1], s1_send.at[1, k - 1], s1_recv.at[1], to)
+    def step1_b(now):
+        @pl.when(now)
+        def _():
+            for k in far_first:
+                to = dev(dz=(1 - c) * k, dy=c * k)
+                send(part1.at[1, (line + k) % 8], recv1.at[1, k - 1], s1_send.at[1], s1_recv.at[1], to)
 
     def step1_half(h):
         rows = pl.ds(64 * h, 64)
         for k in far_first:
             src = part1.at[2, (y + k) % 8, rows]
-            send(src, recv1.at[2, k - 1, rows], s1_send.at[2 + h, k - 1], s1_recv.at[2 + h], dev(dy=k))
+            send(src, recv1.at[2, k - 1, rows], s1_send.at[2], s1_recv.at[2 + h], dev(dy=k))
 
     pl.semaphore_wait(barrier, len(partners))
     fetch(1, 0)
@@ -197,25 +199,25 @@
     part = dot(target[...], kern[0, c], NT)[0:8]
     rpart[...] = part
     forward(1, 0)
-    fetch(2, 0)
-    fetch(2, 1)
+    fetch_c(x != 1)
     hear(1)
     tell(2)
     forward(1, 1)
+    fetch_c(x == 1)
     arrived(kern.at[0, 1 - c], d_recv)
     multiply_a()
     hear(2)
     for k in far_first:
-        send(rpart, rz.at[k - 1], rz_send.at[k - 1], rz_recv, dev(dz=k))
+        send(rpart, rz.at[k - 1], rz_send, rz_recv, dev(dz=k))
     forward(2, 0)
     gathered(1, 0)
     make_rows(1, 0, 128)
     forward(2, 1)
-    step1_a()
+    step1_a(x < 2)
     gathered(1, 1)
     make_rows(1, 128, 128)
     multiply_b()
-    step1_b()
+    step1_b(x != 2)
 
     gathered(2, 0)
     make_rows(2, 0, 128)
@@ -232,18 +234,19 @@
         total = total + jnp.where(slot == 7, part, value)
     rsum[...] = total
     for k in far_first:
-        send(rsum, ry.at[k - 1], ry_send.at[k - 1], ry_recv, dev(dy=k))
+        send(rsum, ry.at[k - 1], ry_send, ry_recv, dev(dy=k))
 
     gathered(2, 1)
     make_rows(2, 128, 128)
     multiply_half(1)
     step1_half(1)
+    step1_b(x == 2)
+    step1_a(x >= 2)
 
     pl.semaphore_wait(token.at[3], 3)
 
     def deliver(n, src, dst, to):
         here = (to[0] == r) & (to[1] == b)
-        copy = remote(src, dst, s2_send.at[n], s2_recv, to)
 
         @pl.when(here)
         def _():
@@ -251,9 +254,7 @@
 
         @pl.when(jnp.logical_not(here))
         def _():
-            copy.start()
-
-        return here, copy
+            send(src, dst, s2_send.at[n], s2_recv, to)
 
     def first_sum(j, mine, rows, sem):
         arrived(recv1.at[j, :, rows], sem)
@@ -272,41 +273,53 @@
     targets_a = [((2 * x + down // 2) * 8 + 4 * (down % 2) + k, 2 * x + across // 2) for k in range(4)]
     targets_t = [((2 * x + across // 2) * 8 + 4 * (across % 2) + k, 2 * x + down // 2) for k in range(4)]
 
-    @pl.when(holds)
-    def _():
-        acc = first_sum(0, n, pl.ds(0, 128), s1_recv.at[0])
-        part2[0] = acc.astype(BF16)
-        for k in range(4):
-            src = part2.at[0, pl.ds(32 * k, 32)]
-            deliver(8 + k, src, recv2.at[across % 2, y], targets_a[k])
-
-        @pl.when(down != across)
-        def _():
-            part2[4] = acc.T.astype(BF16)
+    def step2_a(now):
+        @pl.when(holds & now)
+        def _():
+            acc = first_sum(0, n, pl.ds(0, 128), s1_recv.at[0])
+            part2[0] = acc.astype(BF16)
             for k in range(4):
-                src = part2.at[4, pl.ds(32 * k, 32)]
-                deliver(12 + k, src, recv2.at[down % 2, y], targets_t[k])
+                src = part2.at[0, pl.ds(32 * k, 32)]
+                deliver(0, src, recv2.at[across % 2, y], targets_a[k])
+
+            @pl.when(down != across)
+            def _():
+                part2[4] = acc.T.astype(BF16)
+                for k in range(4):
+                    src = part2.at[4, pl.ds(32 * k, 32)]
+                    deliver(1, src, recv2.at[down % 2, y], targets_t[k])
 
     w, h, a = line // 4, (line // 2) % 2, line % 2
     cross, block = z + y - line, 2 * ((x + 1) % 4) + c
-    acc = first_sum(1, line, pl.ds(0, 128), s1_recv.at[1])
-    part2[1] = acc.astype(BF16)
-    part2[3] = acc.T.astype(BF16)
-    for k in range(4):
-        src = part2.at[3, pl.ds(32 * k, 32)]
-        send(src, recv2.at[h, cross], s2_send.at[k], s2_recv, ((2 * x + a) * 8 + 4 * w + k, block))
-    for k in range(4):
-        src = part2.at[1, pl.ds(32 * k, 32)]
-        local.append(deliver(4 + k, src, recv2.at[w, cross], (block * 8 + 4 * h + k, 2 * x + a)))
-
-    for half in (0, 1):
-        rows = pl.ds(64 * half, 64)
-        part2[2, rows] = first_sum(2, y, rows, s1_recv.at[2 + half]).astype(BF16)
-        for n in range(4):
-            src = part2.at[2, pl.ds(64 * half + 16 * n, 16)]
-            dst = recv2.at[n % 2, z, pl.ds(16 * half, 16)]
-            to = ((2 * ((x + 2) % 4) + c) * 8 + y, 2 * x + n // 2)
-            local.append(deliver(16 + 4 * half + n, src, dst, to))
+
+    def step2_b(now):
+        @pl.when(now)
+        def _():
+            acc = first_sum(1, line, pl.ds(0, 128), s1_recv.at[1])
+            part2[1] = acc.astype(BF16)
+            part2[3] = acc.T.astype(BF16)
+            for k in range(4):
+                src = part2.at[3, pl.ds(32 * k, 32)]
+                send(src, recv2.at[h, cross], s2_send.at[2], s2_recv, ((2 * x + a) * 8 + 4 * w + k, block))
+            for k in range(4):
+                src = part2.at[1, pl.ds(32 * k, 32)]
+                deliver(3, src, recv2.at[w, cross], (block * 8 + 4 * h + k, 2 * x + a))
+
+    def step2_c():
+        for half in (0, 1):
+            rows = pl.ds(64 * half, 64)
+            part2[2, rows] = first_sum(2, y, rows, s1_recv.at[2 + half]).astype(BF16)
+            for n in range(4):
+                src = part2.at[2, pl.ds(64 * half + 16 * n, 16)]
+                dst = recv2.at[n % 2, z, pl.ds(16 * half, 16)]
+                to = ((2 * ((x + 2) % 4) + c) * 8 + y, 2 * x + n // 2)
+                deliver(4, src, dst, to)
+
+    step2_a(x < 2)
+    step2_b(x != 2)
+    step2_c()
+    step2_b(x == 2)
+    step2_a(x >= 2)
 
     arrived(ry, ry_recv)
     final = jnp.zeros((8, PTS), F32)
@@ -316,18 +329,36 @@
         final = final + jnp.where(slot == 7, total, value)
     right_ref[...] = final[0:1] / ROWS_ALL
 
-    for k in range(4):
-        for n, src, to, active in ((8, 0, targets_a[k], holds), (12, 4, targets_t[k], holds & (down != across))):
-            here = (to[0] == r) & (to[1] == b)
-            copy = remote(part2.at[src, pl.ds(32 * k, 32)], recv2.at[0, 0], s2_send.at[n + k], s2_recv, to)
-            local.append((here | jnp.logical_not(active), copy))
-    for copy in sends:
-        copy.wait_send()
-    for here, copy in local:
-
-        @pl.when(jnp.logical_not(here))
-        def _(copy=copy):
-            copy.wait_send()
+    arrived(panel.at[0, pl.ds(0, 128)], x_send)
+    arrived(panel.at[pl.ds(0, 3), pl.ds(0, 128)], f_send)
+    arrived(kern.at[0, c], d_send)
+    arrived(rz, rz_send)
+    arrived(ry, ry_send)
+    arrived(recv1.at[1], s1_send.at[1])
+    arrived(recv1.at[2], s1_send.at[2])
+    arrived(part2.at[2], s2_send.at[2])
+
+    def left(ref, few, many, fewer, sem, active=True):
+        @pl.when(active & fewer)
+        def _():
+            arrived(ref.at[pl.ds(0, few)], sem)
+
+        @pl.when(active & jnp.logical_not(fewer))
+        def _():
+            arrived(ref.at[pl.ds(0, many)], sem)
+
+    def among(targets):
+        found = False
+        for to in targets:
+            found = found | ((to[0] == r) & (to[1] == b))
+        return found
+
+    flat = part2.at[0]
+    left(recv1.at[0], 4, 5, holds, s1_send.at[0])
+    left(flat, 96, 128, among(targets_a), s2_send.at[0], holds)
+    left(flat, 96, 128, among(targets_t), s2_send.at[1], holds & (down != across))
+    left(flat, 96, 128, among([(block * 8 + 4 * h + k, 2 * x + a) for k in range(4)]), s2_send.at[3])
+    left(flat, 64, 128, z == 2 * ((x + 2) % 4) + c, s2_send.at[4])
 
     arrived(recv2, s2_recv)
     for w2 in (0, 1):
@@ -378,19 +409,19 @@
             dma((8, PTS), F32),
             dma((7, 8, PTS), F32),
             sem((8,)),
+            sem,
             sem((2, 2)),
+            sem,
             sem((2, 2)),
-            sem((2, 2, 3)),
-            sem((2, 2)),
-            sem,
-            sem,
-            sem((4, 7)),
+            sem,
+            sem,
+            sem((3,)),
             sem((4,)),
-            sem((24,)),
-            sem,
-            sem((7,)),
-            sem,
-            sem((7,)),
+            sem((5,)),
+            sem,
+            sem,
+            sem,
+            sem,
             sem,
             pltpu.SemaphoreType.REGULAR((4,)),
         ],

time: 42.9 us -> 42.3 us (0.986); the launches traced: 42.2 us -> 42.2 us
  no operation moved by 1% of the time
where the time goes in v4:
time: 42.3 us; the launch traced here: 42.2 us
  Pallas kernels  40.4 us (96%)
  local copies, waits for them, and re-layouts  1.18 us (3%)
  between operations  0.64 us (2%)
    pallas_call x1, Pallas kernels, body(): pl.pallas_call(kernel, out_shape=(jax.ShapeDtypeStruct((32, PTS), F32), j...  40.4 us
    unnamed x2, local copies, waits for them, and re-layouts  1.18 us

profile of v4, /device:TPU:7, one launch (start us, length us, event | category | flops | bytes accessed | tf_op | source)
XLA Modules:
  0.0 42.2 jit_solution(2097555184262357924)
XLA Ops:
  0.6 40.4 %gram.1 = (f32[32,256]{1,0:T(8,128)S(1)}, f32[1,256]{1,0:T(1,128)S(1)}) custom-call(bf16[1000,512]{1,0:T(8,128)(2,1)} %desc_hbm.1, bf16[1000,256]{1,0:T(8,128)(2,1)} %bitcast.8, s32[1,512]{1,0:T(1,128)} %bitcast.10, bf16[1,32]{1,0:T(2,128)(2,1)} %bitcast.12, s32[1,32]{1,0:T(1,128)} %bitcast.13, s32[1,1024]{1,0:T(1,128)} %bitcast.9, ...), custom_call_target="tpu_custom_call" | custom-call | tf_op jit(solution)/shard_map/gram/pallas_call | solution.py:384
  41.0 0.6 %copy.12 = f32[32,256]{1,0:T(8,128)} copy(f32[32,256]{1,0:T(8,128)S(1)} %get-tuple-element.8) | data formatting | bytes 65536
  41.6 0.6 %copy.13 = f32[256]{0:T(256)} copy(f32[256]{0:T(256)S(1)} %bitcast.7) | data formatting | bytes 2048

commit v5 on v4

--- a/solution.py
+++ b/solution.py
@@ -199,11 +199,11 @@
     part = dot(target[...], kern[0, c], NT)[0:8]
     rpart[...] = part
     forward(1, 0)
-    fetch_c(x != 1)
+    fetch_c(x == 0)
     hear(1)
     tell(2)
     forward(1, 1)
-    fetch_c(x == 1)
+    fetch_c(x != 0)
     arrived(kern.at[0, 1 - c], d_recv)
     multiply_a()
     hear(2)
@@ -223,6 +223,7 @@
     make_rows(2, 0, 128)
     multiply_half(0)
     step1_half(0)
+    step1_a(x == 3)
 
     arrived(rz, rz_recv)
     for to in (dev(dc=1), dev(dx=-1), dev(dx=-1, dc=1)):
@@ -241,7 +242,7 @@
     multiply_half(1)
     step1_half(1)
     step1_b(x == 2)
-    step1_a(x >= 2)
+    step1_a(x == 2)
 
     pl.semaphore_wait(token.at[3], 3)
 

time: 42.3 us -> 42.6 us (level)
  no operation moved by 1% of the time
where the time goes in v5:
time: 42.6 us; the launch traced here: 42.5 us
  Pallas kernels  40.6 us (95%)
  local copies, waits for them, and re-layouts  1.18 us (3%)
  between operations  0.64 us (2%)
    pallas_call x1, Pallas kernels, body(): pl.pallas_call(kernel, out_shape=(jax.ShapeDtypeStruct((32, PTS), F32), j...  40.6 us
    unnamed x2, local copies, waits for them, and re-layouts  1.18 us

profile of v5, /device:TPU:7, one launch (start us, length us, event | category | flops | bytes accessed | tf_op | source)
XLA Modules:
  0.0 42.5 jit_solution(1625817077321628359)
XLA Ops:
  0.6 40.6 %gram.1 = (f32[32,256]{1,0:T(8,128)S(1)}, f32[1,256]{1,0:T(1,128)S(1)}) custom-call(bf16[1000,512]{1,0:T(8,128)(2,1)} %desc_hbm.1, bf16[1000,256]{1,0:T(8,128)(2,1)} %bitcast.8, s32[1,512]{1,0:T(1,128)} %bitcast.10, bf16[1,32]{1,0:T(2,128)(2,1)} %bitcast.12, s32[1,32]{1,0:T(1,128)} %bitcast.13, s32[1,1024]{1,0:T(1,128)} %bitcast.9, ...), custom_call_target="tpu_custom_call" | custom-call | tf_op jit(solution)/shard_map/gram/pallas_call | solution.py:385
  41.3 0.6 %copy.12 = f32[32,256]{1,0:T(8,128)} copy(f32[32,256]{1,0:T(8,128)S(1)} %get-tuple-element.8) | data formatting | bytes 65536
  41.9 0.6 %copy.13 = f32[256]{0:T(256)} copy(f32[256]{0:T(256)S(1)} %bitcast.7) | data formatting | bytes 2048

commit v6 on v5

--- a/solution.py
+++ b/solution.py
@@ -51,13 +51,12 @@
         (etarget_hbm, etarget_ref), (ftarget_hbm, ftarget_ref), (desc_hbm, desc), (grad_hbm, grad),
     )
     loads = [pltpu.make_async_copy(src, dst, load_sem.at[n]) for n, (src, dst) in enumerate(copies)]
-    loads[0].start()
     around = [dev(dy=1), dev(dy=-1), dev(dz=1), dev(dz=-1)]
     partners = [dev(dc=1), dev(dx=2)] + [dev(dx=dx, dc=dc) for dx in (1, 3) for dc in (0, 1)] + around
     barrier = pltpu.get_barrier_semaphore()
     for partner in partners:
         pl.semaphore_signal(barrier, inc=1, device_id=partner, device_id_type=MESH)
-    for load in loads[1:]:
+    for load in loads:
         load.start()
     loads[0].wait()
     points = panel_t[...].T
@@ -223,7 +222,6 @@
     make_rows(2, 0, 128)
     multiply_half(0)
     step1_half(0)
-    step1_a(x == 3)
 
     arrived(rz, rz_recv)
     for to in (dev(dc=1), dev(dx=-1), dev(dx=-1, dc=1)):
@@ -242,7 +240,7 @@
     multiply_half(1)
     step1_half(1)
     step1_b(x == 2)
-    step1_a(x == 2)
+    step1_a(x >= 2)
 
     pl.semaphore_wait(token.at[3], 3)
 

time: 42.6 us -> 42.5 us (level)
  no operation moved by 1% of the time
where the time goes in v6:
time: 42.5 us; the launch traced here: 42.4 us
  Pallas kernels  40.6 us (96%)
  local copies, waits for them, and re-layouts  1.18 us (3%)
  between operations  0.64 us (2%)
    pallas_call x1, Pallas kernels, body(): pl.pallas_call(kernel, out_shape=(jax.ShapeDtypeStruct((32, PTS), F32), j...  40.6 us
    unnamed x2, local copies, waits for them, and re-layouts  1.18 us

profile of v6, /device:TPU:7, one launch (start us, length us, event | category | flops | bytes accessed | tf_op | source)
XLA Modules:
  0.0 42.4 jit_solution(10914040846229756797)
XLA Ops:
  0.6 40.6 %gram.1 = (f32[32,256]{1,0:T(8,128)S(1)}, f32[1,256]{1,0:T(1,128)S(1)}) custom-call(bf16[1000,512]{1,0:T(8,128)(2,1)} %desc_hbm.1, bf16[1000,256]{1,0:T(8,128)(2,1)} %bitcast.8, s32[1,512]{1,0:T(1,128)} %bitcast.10, bf16[1,32]{1,0:T(2,128)(2,1)} %bitcast.12, s32[1,32]{1,0:T(1,128)} %bitcast.13, s32[1,1024]{1,0:T(1,128)} %bitcast.9, ...), custom_call_target="tpu_custom_call" | custom-call | tf_op jit(solution)/shard_map/gram/pallas_call | solution.py:383
  41.2 0.6 %copy.12 = f32[32,256]{1,0:T(8,128)} copy(f32[32,256]{1,0:T(8,128)S(1)} %get-tuple-element.8) | data formatting | bytes 65536
  41.8 0.6 %copy.13 = f32[256]{0:T(256)} copy(f32[256]{0:T(256)S(1)} %bitcast.7) | data formatting | bytes 2048
